TPU v7x, 32 devices: a whole 2x2x4 slice. The times are simulated.
32 devices in a mesh: kv: 8 (over y, x, core), tp: 4 (over z).
Axes of the slice: x: 2, y: 2, z: 4, core: 2. Of those that a mesh axis runs over, the one named last changes fastest.
Arguments:
- activations: bfloat16 [64, 5120], P(('kv', 'tp')), may hold values from -27 to 27
- queries: bfloat16 [64, 5120], P('kv', 'tp'), may hold values from -16 to 16
- tree_cache_keys: bfloat16 [8192, 1024], P('kv', 'tp'), may hold values from -16 to 16
- tree_cache_values: bfloat16 [8192, 1024], P('kv', 'tp'), may hold values from -8 to 8
- parents: int32 [13], replicated, may hold values from 0 to 4, as said below
- node_lengths: int32 [13], replicated, may hold values from 1 to 2048, as said below
- token_leaf: int32 [64], replicated, may hold values from 5 to 12
- out_weight: bfloat16 [5120, 5120], P('tp'), may hold values from -0.078125 to 0.078125
- norm_gain: float32 [5120], replicated, may hold values from 0.5 to 1.5
- gate_weight: bfloat16 [5120, 27648], P(None, ('kv', 'tp')), may hold values from -0.078125 to 0.078125
- up_weight: bfloat16 [5120, 27648], P(None, ('kv', 'tp')), may hold values from -0.078125 to 0.078125
- down_weight: bfloat16 [27648, 5120], P(('kv', 'tp')), may hold values from -0.0390625 to 0.0390625
Outputs:
- output: bfloat16 [64, 5120], P(('kv', 'tp'))
Inputs may be any that keep to these rules, and one draw needn't show every extreme that they name: Node 0 is the root, nodes 1 to 4 are tenants, the rest are leaves. parents[0] = 0, every tenant's parent is 0, every leaf's parent is a tenant, and every tenant is the parent of some leaf. `node_lengths`: the root holds exactly 2048 slots, every tenant at most 1024 and one tenant exactly that many, every leaf at most 256 and one leaf exactly that many. The nodes' slots follow one another in node order from slot 0.
All inputs are finite; a program needn't handle non-finite values.
Results may differ from a plain program's by a relative error of at most 0.017.
Values may be sent and summed in bfloat16 or wider, within the bound.
A program may use at most 128 MiB of HBM per device.

v0:
```python
import math

import jax
import jax.numpy as jnp
from jax import lax
from jax.sharding import PartitionSpec as P

QUERY_HEADS = 40
KEY_VALUE_HEADS = 8
HEAD_WIDTH = 128


LOWEST = -1e30
EPSILON = 1e-06


def merged_2(value, axis, combine):
    everything = jax.tree.map(
        lambda part, kind: lax.all_gather(part.astype(kind), axis),
        value,
        jax.tree.map(lambda a: jnp.bfloat16 if a.dtype == jnp.float32 else a.dtype, value),
    )

    def take(k):
        return jax.tree.map(lambda part, own: part[k].astype(own.dtype), everything, value)

    return lax.fori_loop(
        1, lax.axis_size(axis), lambda k, so_far: combine(so_far, take(k)), take(0)
    )


def slot_owner(node_lengths, first_slot, slot_total):
    node_ends = jnp.cumsum(node_lengths)
    node_starts = node_ends - node_lengths
    slot_ids = first_slot + jnp.arange(slot_total, dtype=jnp.int32)
    inside = (slot_ids[:, None] >= node_starts[None, :]) & (slot_ids[:, None] < node_ends[None, :])
    labels = jnp.arange(node_lengths.shape[0], dtype=jnp.int32)
    holder = jnp.sum(jnp.where(inside, labels[None, :], 0), axis=1)
    return jnp.where(jnp.any(inside, axis=1), holder, -1)


def parent_of(node_ids, parents):
    labels = jnp.arange(parents.shape[0], dtype=jnp.int32)
    return jnp.sum(jnp.where(node_ids[:, None] == labels[None, :], parents[None, :], 0), axis=1)


def combine(earlier, later):
    highest = jnp.maximum(earlier[0], later[0])
    weight_early = jnp.exp(earlier[0] - highest)
    weight_late = jnp.exp(later[0] - highest)
    return (
        highest,
        earlier[1] * weight_early + later[1] * weight_late,
        earlier[2] * weight_early[..., None] + later[2] * weight_late[..., None],
    )


def attend_rows(
    carried,
    query_head_rows,
    leaf_ids,
    tenant_ids,
    key_rows,
    value_rows,
    node_lengths,
    first_slot,
    score_scale,
):
    row_total = key_rows.shape[0]
    block_length = math.gcd(row_total, 512)
    count_of_blocks = row_total // block_length
    kv_local = query_head_rows.shape[1]
    head_size = query_head_rows.shape[3]
    slot_node = slot_owner(node_lengths, first_slot, row_total).reshape(
        count_of_blocks, block_length
    )
    key_blocks = key_rows.reshape(count_of_blocks, block_length, kv_local, head_size)
    value_blocks = value_rows.reshape(count_of_blocks, block_length, kv_local, head_size)

    def one_block(running, sliced):
        key_block, value_block, node_block = sliced
        scores = (
            jnp.einsum(
                "tkgd,skd->tkgs", query_head_rows, key_block, preferred_element_type=jnp.float32
            )
            * score_scale
        )
        allowed = (
            (node_block[None, :] == 0)
            | (node_block[None, :] == tenant_ids[:, None])
            | (node_block[None, :] == leaf_ids[:, None])
        )
        allowed = allowed[:, None, None, :]
        highest = jnp.maximum(running[0], jnp.max(jnp.where(allowed, scores, LOWEST), axis=3))
        weights = jnp.exp(jnp.where(allowed, scores - highest[..., None], -jnp.inf))
        shrink = jnp.exp(running[0] - highest)
        denominator = running[1] * shrink + jnp.sum(weights, axis=3)
        weighted = running[2] * shrink[..., None] + jnp.einsum(
            "tkgs,skd->tkgd",
            weights.astype(jnp.bfloat16),
            value_block,
            preferred_element_type=jnp.float32,
        )
        return ((highest, denominator, weighted), None)

    result, unused = lax.scan(one_block, carried, (key_blocks, value_blocks, slot_node))
    return result


def local(
    activations,
    queries,
    tree_cache_keys,
    tree_cache_values,
    parents,
    node_lengths,
    token_leaf,
    out_weight,
    norm_gain,
    gate_weight,
    up_weight,
    down_weight,
):
    head_size = HEAD_WIDTH
    heads_per_group = QUERY_HEADS // KEY_VALUE_HEADS
    kv_local = tree_cache_keys.shape[1] // head_size
    tok_group = queries.shape[0]
    keys_local = tree_cache_keys.shape[0]
    score_scale = 1.0 / math.sqrt(head_size)
    group_index = lax.axis_index("kv")
    tenant_all = parent_of(token_leaf, parents)
    gathered = lax.all_gather(queries, "kv", axis=0, tiled=True)
    all_heads = gathered.reshape(gathered.shape[0], kv_local, heads_per_group, head_size)
    row_count = gathered.shape[0]
    partial_value = attend_rows(
        (
            jnp.full((row_count, kv_local, heads_per_group), LOWEST, jnp.float32),
            jnp.zeros((row_count, kv_local, heads_per_group), jnp.float32),
            jnp.zeros((row_count, kv_local, heads_per_group, head_size), jnp.float32),
        ),
        all_heads,
        token_leaf,
        tenant_all,
        tree_cache_keys,
        tree_cache_values,
        node_lengths,
        group_index * keys_local,
        score_scale,
    )
    merged = merged_2(partial_value, "kv", combine)
    highest, denominator, weighted = [
        lax.dynamic_slice_in_dim(member, group_index * tok_group, tok_group, 0) for member in merged
    ]
    context = (
        (weighted / denominator[..., None])
        .astype(jnp.bfloat16)
        .reshape(tok_group, kv_local * heads_per_group * head_size)
    )
    picked = context
    attended = lax.psum_scatter(
        jnp.dot(picked, out_weight, preferred_element_type=jnp.float32).astype(jnp.bfloat16),
        "tp",
        scatter_dimension=0,
        tiled=True,
    ).astype(jnp.float32)
    residual = (activations.astype(jnp.float32) + attended).astype(jnp.bfloat16)
    widened = residual.astype(jnp.float32)
    normed = (
        widened
        * lax.rsqrt(jnp.mean(widened * widened, axis=1, keepdims=True) + EPSILON)
        * norm_gain
    ).astype(jnp.bfloat16)
    piece = lax.all_gather(normed, ("kv", "tp"), axis=0, tiled=True)
    gate_proj = jnp.dot(piece, gate_weight, preferred_element_type=jnp.float32)
    up_proj = jnp.dot(piece, up_weight, preferred_element_type=jnp.float32)
    hidden = (jax.nn.silu(gate_proj) * up_proj).astype(jnp.bfloat16)
    picked = hidden
    mixed = lax.psum_scatter(
        jnp.dot(picked, down_weight, preferred_element_type=jnp.float32),
        ("kv", "tp"),
        scatter_dimension=0,
        tiled=True,
    )
    return (widened + mixed).astype(jnp.bfloat16)


def solution(mesh):
    return jax.shard_map(
        local,
        mesh=mesh,
        in_specs=(
            P(("kv", "tp"), None),
            P("kv", "tp"),
            P("kv", "tp"),
            P("kv", "tp"),
            P(),
            P(),
            P(),
            P("tp", None),
            P(),
            P(None, ("kv", "tp")),
            P(None, ("kv", "tp")),
            P(("kv", "tp"), None),
        ),
        out_specs=P(("kv", "tp"), None),
        check_vma=False,
    )
```

profile of v0, /device:TPU:0, one launch (start us, length us, event | category | flops | bytes accessed | tf_op | source)
XLA Modules:
  0.0 332.7 jit_solution(4950036565610489889)
XLA Ops:
  6.5 0.9 reduce-window.8
  7.5 0.7 bitcast_subtract_fusion
  8.4 10.9 %all_gather.24 = bf16[64,1280]{1,0:T(8,128)(2,1)S(1)} all-gather(bf16[8,1280]{1,0:T(8,128)(2,1)} %param.17), channel_id=1, replica_groups=mesh['kv'=8,'tp'=4] {'kv'}, dimensions={0}, use_global_device_ids=true | all-gather | bytes 184320 | tf_op jit(solution)/shard_map/all_gather | solution.py:132
  19.3 0.2 reshape.138
  19.6 0.1 reshape.137
  19.7 0.1 reshape.139
  19.8 0.3 copy-done.4
  20.2 3.8 %while.35 = (s32[]{:T(128)}, f32[64,2,5]{0,2,1:T(8,128)S(1)}, f32[64,2,5]{0,2,1:T(8,128)S(1)}, f32[64,2,5,128]{3,0,2,1:T(8,128)S(1)}, s32[2,512]{1,0:T(2,128)S(1...) while((s32[]{:T(128)}, f32[64,2,5]{0,2,1:T(8,128)S(1)}, ...), condition=%wide.region_7.8_spmd.clone, body=%wide.region_4.7_spmd.clone.sunk | while | flops 171101824 | bytes 6504073 | solution.py:106
  20.4 0.4 constant_dynamic-slice_fusion.9
  20.8 0.4 select_reduce_fusion.4
  21.2 0.4 fusion.49
  21.6 0.5 fusion.51
  22.3 0.4 constant_dynamic-slice_fusion.9
  22.7 0.4 select_reduce_fusion.4
  23.1 0.4 fusion.49
  23.5 0.5 fusion.51
  24.0 0.7 convert_element_type.103
  24.8 0.1 copy.77
  24.9 9.1 %all-gather = bf16[512,2,5]{2,1,0:T(2,128)(2,1)S(1)} all-gather(bf16[64,2,5]{2,1,0:T(2,128)(2,1)S(1)} %copy.77), channel_id=2, replica_groups=mesh['kv'=8,'tp'=4] {'kv'}, dimensions={0}, use_global_device_ids=true | all-gather | bytes 11520 | tf_op jit(solution)/shard_map/all_gather | solution.py:19
  34.2 0.1 copy.79
  34.3 8.5 %all-gather.1 = bf16[512,2,5]{2,1,0:T(2,128)(2,1)S(1)} all-gather(bf16[64,2,5]{2,1,0:T(2,128)(2,1)S(1)} %copy.79), channel_id=3, replica_groups=mesh['kv'=8,'tp'=4] {'kv'}, dimensions={0}, use_global_device_ids=true | all-gather | bytes 11520 | tf_op jit(solution)/shard_map/all_gather | solution.py:19
  42.9 0.2 copy.85
  43.1 0.2 copy.86
  43.3 6.5 %all-gather.6.cloned.1.call-done = bf16[512,2,5,128]{3,0,2,1:T(8,128)(2,1)} async-done(((bf16[64,2,5,128]{3,0,2,1:T(8,128)(2,1)}), bf16[512,2,5,128]{3,0,2,1:T(8,128)(2,1)}) %all-gather.6.cloned.1.call-update) | async-done | bytes 1310736 | tf_op jit(solution)/shard_map/all_gather | solution.py:19
  49.8 0.9 slice_convert_fusion
  50.7 0.2 copy.84
  50.9 12.6 %while.34 = (s32[]{:T(128)}, f32[64,2,5]{0,1,2:T(2,128)S(1)}, f32[64,2,5]{0,1,2:T(2,128)S(1)}, f32[64,2,5,128]{3,2,1,0:T(8,128)S(1)}, bf16[8,64,2,5]{1,2,3,0:T(2...) while((s32[]{:T(128)}, f32[64,2,5]{0,1,2:T(2,128)S(1)}, ...), condition=%wide.region_9.10_spmd, body=%wide.region_8.9_spmd.sunk | while | flops 332805 | bytes 1180311 | solution.py:27
  51.0 0.1 copy.118
  51.1 0.1 copy.119
  51.2 0.9 constant_dynamic-slice_fusion.8
  52.2 0.5 fusion.46
  52.8 0.1 copy.118
  52.9 0.1 copy.119
  53.0 0.9 constant_dynamic-slice_fusion.8
  54.0 0.5 fusion.46
  54.6 0.1 copy.118
  54.7 0.1 copy.119
  54.8 0.9 constant_dynamic-slice_fusion.8
  55.8 0.5 fusion.46
  56.4 0.1 copy.118
  56.5 0.1 copy.119
  56.6 0.9 constant_dynamic-slice_fusion.8
  57.6 0.5 fusion.46
  58.2 0.1 copy.118
  58.3 0.1 copy.119
  58.4 0.9 constant_dynamic-slice_fusion.8
  59.4 0.5 fusion.46
  60.0 0.1 copy.118
  60.1 0.1 copy.119
  60.2 0.9 constant_dynamic-slice_fusion.8
  61.2 0.5 fusion.46
  61.9 0.1 copy.119
  62.0 0.9 constant_dynamic-slice_fusion.8
  63.0 0.5 fusion.46
  63.8 7.2 %convolution_convert_fusion = bf16[8,5120]{1,0:T(8,128)(2,1)} fusion(bf16[8,1280]{1,0:T(8,128)(2,1)S(1)} %bitcast.71, bf16[1280,5120]{1,0:T(8,128)(2,1)} %param.23), kind=kOutput, calls=%fused_computation.34 | convolution fusion | flops 104898560 | bytes 13209600 | tf_op jit(solution)/shard_map/dot_general | solution.py:161
  71.1 0.6 dynamic-slice
  72.3 32.8 %all-reduce.5.cloned.1.call-done = bf16[8,5120]{1,0:T(8,128)(2,1)} async-done(((bf16[8,5120]{1,0:T(8,128)(2,1)}), bf16[8,5120]{1,0:T(8,128)(2,1)}) %all-reduce.5.cloned.1.call-update) | async-done | bytes 81936
  105.2 1.0 fusion.22
  106.3 71.0 %all-gather.3 = bf16[32,2,5120]{2,1,0:T(2,128)(2,1)S(1)} all-gather(bf16[1,2,5120]{2,1,0:T(2,128)(2,1)S(1)} %fusion.26), channel_id=1, replica_groups=mesh['kv'=8,'tp'=4] {'kv','tp'}, dimensions={0}, use_global_device_ids=true | all-gather | bytes 675840 | tf_op jit(solution)/shard_map/all_gather | solution.py:173
  177.4 0.2 reshape.160
  177.6 6.2 %fusion.29 = f32[64,864]{1,0:T(8,128)S(1)} fusion(bf16[64,5120]{1,0:T(8,128)(2,1)S(1)} %reshape.160, bf16[5120,864]{0,1:T(8,128)(2,1)} %param.25), kind=kOutput, calls=%fused_computation.68 | convolution fusion | flops 566231040 | bytes 9723904 | tf_op jit(solution)/shard_map/dot_general | solution.py:174
  183.9 12.1 %fusion.14 = f32[64,5120]{1,0:T(8,128)} fusion(bf16[864,5120]{1,0:T(8,128)(2,1)} %param.27, bf16[64,5120]{1,0:T(8,128)(2,1)S(1)} %reshape.160, bf16[5120,864]{0,1:T(8,128)(2,1)} %param.26, f32[64,864]{1,0:T(8,128)S(1)} %fusion.29), kind=kOutput, calls=%fused_computation.37 | convolution fusion | flops 1132793856 | bytes 19881984 | tf_op jit(solution)/shard_map/dot_general | solution.py:179
  196.0 128.7 %all-reduce.7.cloned.1.call-done = f32[64,5120]{1,0:T(8,128)} async-done(((f32[64,5120]{1,0:T(8,128)}), f32[64,5120]{1,0:T(8,128)}) %all-reduce.7.cloned.1.call-update) | async-done | bytes 1310736
  324.6 1.6 fusion.25
  (59 shorter events, 1.8 us)
Async XLA Ops:
  6.5 13.0 %copy-start = (bf16[1024,256]{1,0:T(8,128)(2,1)S(1)}, bf16[1024,256]{1,0:T(8,128)(2,1)}, u32[]{:S(2)}) copy-start(bf16[1024,256]{1,0:T(8,128)(2,1)} %param.18) | copy-start | bytes 1572868
  6.5 13.2 %copy-start.1 = (bf16[1024,256]{1,0:T(8,128)(2,1)S(1)}, bf16[1024,256]{1,0:T(8,128)(2,1)}, u32[]{:S(2)}) copy-start(bf16[1024,256]{1,0:T(8,128)(2,1)} %param.19) | copy-start | bytes 1572868
  6.5 43.2 %all-gather.6.cloned.1.call-start = ((), (), s32[]{:S(2)}) async-start(), calls=%async_computation | async-start | bytes 1474560 | tf_op jit(solution)/shard_map/all_gather | solution.py:19
  19.5 0.7 copy-start.4
  19.5 0.7 copy-start.5
  24.8 80.4 %all-reduce.5.cloned.1.call-start = ((), (), s32[]{:S(2)}) async-start(), calls=%async_computation.1 | async-start | bytes 163840
  63.8 7.3 %copy-start.6 = (u32[32]{0:T(128)S(1)}, u32[32]{0:T(128)}, u32[]{:S(2)}) copy-start(u32[32]{0:T(128)} %constant.93) | copy-start | bytes 388
  63.8 41.4 %copy-start.2 = (bf16[2,5120]{1,0:T(2,128)(2,1)S(1)}, bf16[2,5120]{1,0:T(2,128)(2,1)}, u32[]{:S(2)}) copy-start(bf16[2,5120]{1,0:T(2,128)(2,1)} %param.16) | copy-start | bytes 61444
  63.8 42.4 %copy-start.3 = (f32[5120]{0:T(1024)S(1)}, f32[5120]{0:T(1024)}, u32[]{:S(2)}) copy-start(f32[5120]{0:T(1024)} %param.24) | copy-start | bytes 61444
  71.0 253.6 %all-reduce.7.cloned.1.call-start = ((), (), s32[]{:S(2)}) async-start(), calls=%async_computation.2 | async-start | bytes 2621440
Sparse Core Ops, SparseCore 0:
  24.9 24.8 all-gather.5
  71.1 33.9 all-reduce.4
  196.1 128.4 all-reduce.6
where the time goes:
time: 333 us
  waiting for transfers between devices  168 us (50%)
  blocking collectives  99.5 us (30%)
  matrix products  27.3 us (8%)
  between operations  14 us (4%)
  local copies, waits for them, and re-layouts  11.8 us (4%)
  other arithmetic  11.5 us (3%)
    unnamed x5, waiting for transfers between devices  162 us
    all_gather x1, blocking collectives, local(): piece = lax.all_gather(normed, ('kv', 'tp'), axis=0, tiled=True)  71 us
    all_gather x2, blocking collectives, merged_2(): lax.all_gather(part.astype(kind), axis)  17.6 us
    dot_general x1, matrix products, local(): jnp.dot(picked, down_weight, preferred_element_type=jnp.float32)  12.1 us
    all_gather x1, blocking collectives, local(): gathered = lax.all_gather(queries, 'kv', axis=0, tiled=True)  10.9 us
    dot_general x1, matrix products, local(): jnp.dot(picked, out_weight, preferred_element_type=jnp.float32)  7.16 us
  transfers between devices with their start and end apart: 3, of which 3 were waited for; matrix products, arithmetic and copies ran while one was open for 0% of the time, Pallas kernels for 0%

commit v1 on v0

v1 whole, which is shorter than its diff:
```python
import functools
import math

import jax
import jax.numpy as jnp
from jax import lax
from jax.experimental import pallas as pl
from jax.experimental.pallas import tpu as pltpu
from jax.sharding import PartitionSpec as P

QUERY_HEADS = 40
KEY_VALUE_HEADS = 8
HEAD_WIDTH = 128
LOWEST = -1e30
EPSILON = 1e-06
MESH = pl.DeviceIdType.MESH
F32 = jnp.float32
BF16 = jnp.bfloat16


def copy_to(source, target, send, receive, axis, peer):
    return pltpu.make_async_remote_copy(
        src_ref=source,
        dst_ref=target,
        send_sem=send,
        recv_sem=receive,
        device_id={axis: peer},
        device_id_type=MESH,
    )


def layer_kernel(
    nk,
    nt,
    parts,
    parents,
    lengths,
    leaf_row,
    act,
    query,
    gain,
    keys_hbm,
    values_hbm,
    out_hbm,
    gate_hbm,
    up_hbm,
    down_hbm,
    result,
    keys,
    values,
    out_w,
    gate_w,
    up_w,
    down_w,
    q_all,
    act_all,
    w_send,
    w_recv,
    ml_send,
    ml_recv,
    p_send,
    p_recv,
    res,
    normed,
    acc_gate,
    acc_up,
    s_send,
    s_recv,
    f_send,
    f_recv,
    own,
    load_sem,
    q_ss,
    q_rs,
    a_ss,
    a_rs,
    w_ss,
    w_rs,
    ml_ss,
    ml_rs,
    p_ss,
    p_rs,
    rt_ss,
    rt_rs,
    rk_ss,
    rk_rs,
    s_ss,
    s_rs,
    f_ss,
    f_rs,
):
    k_me = lax.axis_index("kv")
    t_me = lax.axis_index("tp")
    group, q_width = query.shape
    tokens = nk * group
    slots = keys.shape[0]
    kv_local = keys.shape[1] // HEAD_WIDTH
    per_kv = QUERY_HEADS // KEY_VALUE_HEADS
    width = act.shape[1]
    rows_own = act.shape[0]
    cols = width // nt

    loads = [
        pltpu.make_async_copy(source, target, load_sem.at[i])
        for i, (source, target) in enumerate(
            (
                (keys_hbm, keys),
                (values_hbm, values),
                (out_hbm, out_w),
                (gate_hbm, gate_w),
                (up_hbm, up_w),
                (down_hbm, down_w),
            )
        )
    ]
    for load in loads:
        load.start()

    q_all[k_me] = query[...]
    act_all[t_me] = act[...].astype(F32)

    barrier = pltpu.get_barrier_semaphore()
    for d in range(1, nk):
        pl.semaphore_signal(
            barrier, inc=1, device_id={"kv": lax.rem(k_me + d, nk)}, device_id_type=MESH
        )
    for d in range(1, nt):
        pl.semaphore_signal(
            barrier, inc=1, device_id={"tp": lax.rem(t_me + d, nt)}, device_id_type=MESH
        )
    pl.semaphore_wait(barrier, nk + nt - 2)

    kv_to = [lax.rem(k_me + d, nk) for d in range(nk)]
    kv_from = [lax.rem(k_me + nk - d, nk) for d in range(nk)]
    tp_to = [lax.rem(t_me + d, nt) for d in range(nt)]
    tp_from = [lax.rem(t_me + nt - d, nt) for d in range(nt)]
    sends = []

    def send(*args):
        copy = copy_to(*args)
        copy.start()
        sends.append(copy)

    for d in range(1, nk):
        send(q_all.at[k_me], q_all.at[k_me], q_ss.at[d], q_rs.at[d], "kv", kv_to[d])
    for d in range(1, nt):
        send(act_all.at[t_me], act_all.at[t_me], a_ss.at[d], a_rs.at[d], "tp", tp_to[d])

    slot_id = k_me * slots + lax.broadcasted_iota(jnp.int32, (1, slots), 1)
    node = jnp.zeros((1, slots), jnp.int32)
    end = jnp.int32(0)
    nodes = parents.shape[0]
    for n in range(nodes):
        end = end + lengths[n]
        node = node + jnp.where(slot_id >= end, 1, 0)
    node = jnp.where(node == nodes, -1, node)
    diagonal = lax.broadcasted_iota(jnp.int32, (tokens, tokens), 0) == lax.broadcasted_iota(
        jnp.int32, (tokens, tokens), 1
    )
    leaf = jnp.sum(
        jnp.where(diagonal, jnp.broadcast_to(leaf_row[...], (tokens, tokens)), 0),
        axis=1,
        keepdims=True,
    )
    tenant = jnp.zeros_like(leaf)
    for n in range(nodes):
        tenant = tenant + jnp.where(leaf == n, parents[n], 0)
    allowed = ((node == 0) | (node == tenant) | (node == leaf))[None]

    loads[0].wait()
    loads[1].wait()
    for d in range(1, nk):
        block = q_all.at[kv_from[d]]
        copy_to(block, block, q_ss.at[d], q_rs.at[d], "kv", kv_to[d]).wait_recv()

    lane = lax.broadcasted_iota(jnp.int32, (tokens, HEAD_WIDTH), 1)
    tops = jnp.zeros((tokens, HEAD_WIDTH), F32)
    sums = jnp.ones((tokens, HEAD_WIDTH), F32)
    for j in range(kv_local):
        stacked = jnp.concatenate(
            [
                q_all[:, :, h * HEAD_WIDTH : (h + 1) * HEAD_WIDTH]
                .astype(F32)
                .reshape(tokens, HEAD_WIDTH)
                for h in range(j * per_kv, (j + 1) * per_kv)
            ],
            axis=0,
        ).astype(BF16)
        head = slice(j * HEAD_WIDTH, (j + 1) * HEAD_WIDTH)
        scores = lax.dot_general(
            stacked, keys[:, head], (((1,), (1,)), ((), ())), preferred_element_type=F32
        ) * (1.0 / math.sqrt(HEAD_WIDTH))
        scores = scores.reshape(per_kv, tokens, slots)
        top = jnp.max(jnp.where(allowed, scores, LOWEST), axis=2, keepdims=True)
        weights = jnp.where(allowed, jnp.exp(jnp.minimum(scores - top, 0.0)), 0.0)
        total = jnp.sum(weights, axis=2, keepdims=True)
        weighted = jnp.dot(
            weights.astype(BF16).reshape(per_kv * tokens, slots),
            values[:, head],
            preferred_element_type=F32,
        ).reshape(per_kv, nk, group, HEAD_WIDTH)
        for g in range(per_kv):
            h = j * per_kv + g
            w_send[:, :, h * HEAD_WIDTH : (h + 1) * HEAD_WIDTH] = weighted[g].astype(BF16)
            tops = jnp.where(lane == h, top[g], tops)
            sums = jnp.where(lane == h, total[g], sums)
    ml_send[:, 0] = tops.reshape(nk, group, HEAD_WIDTH)
    ml_send[:, 1] = sums.reshape(nk, group, HEAD_WIDTH)

    for d in range(1, nk):
        send(ml_send.at[kv_to[d]], ml_recv.at[d], ml_ss.at[d], ml_rs.at[d], "kv", kv_to[d])
        send(w_send.at[kv_to[d]], w_recv.at[d], w_ss.at[d], w_rs.at[d], "kv", kv_to[d])
    ml_recv[0] = ml_send[k_me]
    w_recv[0] = w_send[k_me]
    loads[2].wait()
    for d in range(1, nk):
        copy_to(
            ml_send.at[kv_to[d]], ml_recv.at[d], ml_ss.at[d], ml_rs.at[d], "kv", kv_to[d]
        ).wait_recv()
        copy_to(
            w_send.at[kv_to[d]], w_recv.at[d], w_ss.at[d], w_rs.at[d], "kv", kv_to[d]
        ).wait_recv()
    highest = ml_recv[0, 0]
    for d in range(1, nk):
        highest = jnp.maximum(highest, ml_recv[d, 0])
    scales = [jnp.exp(ml_recv[d, 0] - highest) for d in range(nk)]
    denominator = scales[0] * ml_recv[0, 1]
    for d in range(1, nk):
        denominator = denominator + scales[d] * ml_recv[d, 1]
    pieces = []
    for h in range(kv_local * per_kv):
        total = jnp.zeros((group, HEAD_WIDTH), F32)
        for d in range(nk):
            part = w_recv[d, :, h * HEAD_WIDTH : (h + 1) * HEAD_WIDTH].astype(F32)
            total = total + part * scales[d][:, h : h + 1]
        pieces.append(total / denominator[:, h : h + 1])
    context = jnp.concatenate(pieces, axis=1).astype(BF16)

    for d in list(range(1, nt)) + [0]:
        at = pl.multiple_of(tp_to[d] * cols, 128)
        product = jnp.dot(context, out_w[:, pl.ds(at, cols)], preferred_element_type=F32)
        if d > 0:
            p_send[d] = product.astype(BF16)
            send(p_send.at[d], p_recv.at[d], p_ss.at[d], p_rs.at[d], "tp", tp_to[d])
    for d in range(1, nt):
        block = act_all.at[tp_from[d]]
        copy_to(block, block, a_ss.at[d], a_rs.at[d], "tp", tp_to[d]).wait_recv()
    mine = pl.ds(pl.multiple_of(t_me * cols, 128), cols)
    row = lax.broadcasted_iota(jnp.int32, (group, cols), 0)
    before = jnp.zeros((group, cols), F32)
    for t in range(nt):
        block = act_all[t, :, mine]
        for i in range(rows_own):
            before = jnp.where(
                row == t * rows_own + i, jnp.broadcast_to(block[i : i + 1], (group, cols)), before
            )
    attended = product
    for d in range(1, nt):
        copy_to(
            p_send.at[d], p_recv.at[d], p_ss.at[d], p_rs.at[d], "tp", tp_to[d]
        ).wait_recv()
        attended = attended + p_recv[d].astype(F32)
    res[k_me, t_me] = (before + attended).astype(BF16)

    for d in range(1, nt):
        block = res.at[k_me, t_me]
        send(block, block, rt_ss.at[d], rt_rs.at[d], "tp", tp_to[d])
    for d in range(1, nt):
        block = res.at[k_me, tp_from[d]]
        copy_to(block, block, rt_ss.at[d], rt_rs.at[d], "tp", tp_to[d]).wait_recv()
    for d in range(1, nk):
        send(res.at[k_me], res.at[k_me], rk_ss.at[d], rk_rs.at[d], "kv", kv_to[d])
    loads[3].wait()
    loads[4].wait()
    loads[5].wait()
    acc_gate[...] = jnp.zeros_like(acc_gate)
    acc_up[...] = jnp.zeros_like(acc_up)
    for d in range(1, nk):
        block = res.at[kv_from[d]]
        copy_to(block, block, rk_ss.at[d], rk_rs.at[d], "kv", kv_to[d]).wait_recv()

    for p in range(nk // 2):
        pair = [
            res[2 * p : 2 * p + 2, c].astype(F32).reshape(2 * group, cols) for c in range(nt)
        ]
        square = sum(jnp.sum(part * part, axis=1, keepdims=True) for part in pair)
        inverse = lax.rsqrt(square / width + EPSILON)
        for c in range(nt):
            at = slice(c * cols, (c + 1) * cols)
            normed[2 * p * group : 2 * (p + 1) * group, at] = (
                pair[c] * inverse * gain[:, at]
            ).astype(BF16)

    step = 640

    @pl.loop(0, width // step)
    def _(i):
        at = pl.ds(pl.multiple_of(i * step, 128), step)
        x = normed[:, at]
        acc_gate[...] += jnp.dot(x, gate_w[at, :], preferred_element_type=F32)
        acc_up[...] += jnp.dot(x, up_w[at, :], preferred_element_type=F32)

    gate = acc_gate[...]
    hidden = (gate / (1.0 + jnp.exp(-gate)) * acc_up[...]).astype(BF16)

    chunk = width // parts
    for c in range(parts):
        at = slice(c * chunk, (c + 1) * chunk)
        product = jnp.dot(hidden, down_w[:, at], preferred_element_type=F32)
        s_send[c] = product.reshape(nk, group, chunk).astype(BF16)
        for d in range(1, nk):
            send(
                s_send.at[c, kv_to[d]],
                s_recv.at[c, d],
                s_ss.at[c, d],
                s_rs.at[c, d],
                "kv",
                kv_to[d],
            )

    row = lax.broadcasted_iota(jnp.int32, (group, cols), 0)
    for c in range(parts):
        at = slice(c * chunk, (c + 1) * chunk)
        mixed = s_send[c, k_me].astype(F32)
        for d in range(1, nk):
            copy_to(
                s_send.at[c, kv_to[d]],
                s_recv.at[c, d],
                s_ss.at[c, d],
                s_rs.at[c, d],
                "kv",
                kv_to[d],
            ).wait_recv()
            mixed = mixed + s_recv[c, d].astype(F32)
        for t in range(nt):
            f_send[c, t] = mixed[t * rows_own : (t + 1) * rows_own].astype(BF16)
        for d in range(1, nt):
            send(
                f_send.at[c, tp_to[d]],
                f_recv.at[c, d],
                f_ss.at[c, d],
                f_rs.at[c, d],
                "tp",
                tp_to[d],
            )
        for b in range(chunk // cols):
            first = c * (chunk // cols) + b
            here = mixed[:, b * cols : (b + 1) * cols] + res[k_me, first].astype(F32)
            for i in range(rows_own):
                own[i : i + 1, first * cols : (first + 1) * cols] = jnp.sum(
                    jnp.where(row == t_me * rows_own + i, here, 0.0), axis=0, keepdims=True
                )
    for c in range(parts):
        at = slice(c * chunk, (c + 1) * chunk)
        total = own[:, at]
        for d in range(1, nt):
            copy_to(
                f_send.at[c, tp_to[d]],
                f_recv.at[c, d],
                f_ss.at[c, d],
                f_rs.at[c, d],
                "tp",
                tp_to[d],
            ).wait_recv()
            total = total + f_recv[c, d].astype(F32)
        result[:, at] = total.astype(BF16)
    for copy in sends:
        copy.wait_send()


def local(
    nk,
    nt,
    activations,
    queries,
    tree_cache_keys,
    tree_cache_values,
    parents,
    node_lengths,
    token_leaf,
    out_weight,
    norm_gain,
    gate_weight,
    up_weight,
    down_weight,
):
    group, q_width = queries.shape
    rows_own, width = activations.shape
    tokens = nk * group
    cols = width // nt
    units = gate_weight.shape[1]
    parts = 2
    chunk = width // parts
    dma = pltpu.SemaphoreType.DMA
    vmem = pl.BlockSpec(memory_space=pltpu.VMEM)
    smem = pl.BlockSpec(memory_space=pltpu.SMEM)
    anywhere = pl.BlockSpec(memory_space=pl.ANY)
    return pl.pallas_call(
        functools.partial(layer_kernel, nk, nt, parts),
        out_shape=jax.ShapeDtypeStruct((rows_own, width), BF16),
        in_specs=[smem, smem, vmem, vmem, vmem, vmem] + [anywhere] * 6,
        out_specs=vmem,
        scratch_shapes=[
            pltpu.VMEM(tree_cache_keys.shape, BF16),
            pltpu.VMEM(tree_cache_values.shape, BF16),
            pltpu.VMEM(out_weight.shape, BF16),
            pltpu.VMEM(gate_weight.shape, BF16),
            pltpu.VMEM(up_weight.shape, BF16),
            pltpu.VMEM(down_weight.shape, BF16),
            pltpu.VMEM((nk, group, q_width), BF16),
            pltpu.VMEM((nt, rows_own, width), F32),
            pltpu.VMEM((nk, group, q_width), BF16),
            pltpu.VMEM((nk, group, q_width), BF16),
            pltpu.VMEM((nk, 2, group, HEAD_WIDTH), F32),
            pltpu.VMEM((nk, 2, group, HEAD_WIDTH), F32),
            pltpu.VMEM((nt, group, cols), BF16),
            pltpu.VMEM((nt, group, cols), BF16),
            pltpu.VMEM((nk, nt, group, cols), BF16),
            pltpu.VMEM((tokens, width), BF16),
            pltpu.VMEM((tokens, units), F32),
            pltpu.VMEM((tokens, units), F32),
            pltpu.VMEM((parts, nk, group, chunk), BF16),
            pltpu.VMEM((parts, nk, group, chunk), BF16),
            pltpu.VMEM((parts, nt, rows_own, chunk), BF16),
            pltpu.VMEM((parts, nt, rows_own, chunk), BF16),
            pltpu.VMEM((rows_own, width), F32),
            dma((6,)),
            dma((nk,)),
            dma((nk,)),
            dma((nt,)),
            dma((nt,)),
            dma((nk,)),
            dma((nk,)),
            dma((nk,)),
            dma((nk,)),
            dma((nt,)),
            dma((nt,)),
            dma((nt,)),
            dma((nt,)),
            dma((nk,)),
            dma((nk,)),
            dma((parts, nk)),
            dma((parts, nk)),
            dma((parts, nt)),
            dma((parts, nt)),
        ],
        compiler_params=pltpu.CompilerParams(
            collective_id=0, has_side_effects=True, vmem_limit_bytes=58 * 2**20
        ),
        name="layer",
    )(
        parents,
        node_lengths,
        token_leaf.reshape(1, tokens),
        activations,
        queries,
        norm_gain.reshape(1, width),
        tree_cache_keys,
        tree_cache_values,
        out_weight,
        gate_weight,
        up_weight,
        down_weight,
    )


def solution(mesh):
    return jax.shard_map(
        functools.partial(local, mesh.shape["kv"], mesh.shape["tp"]),
        mesh=mesh,
        in_specs=(
            P(("kv", "tp"), None),
            P("kv", "tp"),
            P("kv", "tp"),
            P("kv", "tp"),
            P(),
            P(),
            P(),
            P("tp", None),
            P(),
            P(None, ("kv", "tp")),
            P(None, ("kv", "tp")),
            P(("kv", "tp"), None),
        ),
        out_specs=P(("kv", "tp"), None),
        check_vma=False,
    )
```

time: 333 us -> 79.5 us (0.24)
  waiting for transfers between devices: 168 us -> 0 us
  blocking collectives: 99.5 us -> 0 us
  Pallas kernels: 0 us -> 52 us
  matrix products: 27.3 us -> 0 us
  local copies, waits for them, and re-layouts: 11.8 us -> 26.7 us
  between operations: 14 us -> 0.01 us
  other arithmetic: 11.5 us -> 0 us
    unnamed x5 -> x0, waiting for transfers between devices: 162 us -> none
    all_gather x4 -> x0, blocking collectives: 99.5 us -> none  [the longest x1 71 us: local(): piece = lax.all_gather(normed, ('kv', 'tp'), axis=0, tiled=True)]
    pallas_call x0 -> x1, Pallas kernels: none -> 52 us  [local(): pl.pallas_call(functools.partial(layer_kernel, nk, nt, parts), out_shape=...]
    dot_general x7 -> x0, matrix products: 27.3 us -> none  [the longest x1 12.1 us: local(): jnp.dot(picked, down_weight, preferred_element_type=jnp.float32)]
    unnamed x17 -> x3, local copies, waits for them, and re-layouts: 1.23 us -> 26.7 us
    dynamic_slice x11 -> x0, local copies, waits for them, and re-layouts: 7.4 us -> none  [the longest x7 6.58 us: take(): part[k].astype(own.dtype)]
    all_gather x1 -> x0, waiting for transfers between devices: 6.5 us -> none  [merged_2(): lax.all_gather(part.astype(kind), axis)]
    add x17 -> x0, other arithmetic: 4.09 us -> none  [the longest x7 3.81 us: combine(): earlier[2] * weight_early[..., None] + later[2] * weight_late[..., None]]
  transfers between devices with their start and end apart: 3 -> 0, of which waited for: 3 -> 0; matrix products, arithmetic and copies ran while one was open for 0% -> 0% of each run, Pallas kernels for 0% -> 0%
where the time goes in v1:
time: 79.5 us; the launch traced here: 78.7 us
  Pallas kernels  52 us (65%)
  local copies, waits for them, and re-layouts  26.7 us (34%)
    pallas_call x1, Pallas kernels, local(): pl.pallas_call(functools.partial(layer_kernel, nk, nt, parts), out_shape=...  52 us
    unnamed x3, local copies, waits for them, and re-layouts  26.7 us

profile of v1, /device:TPU:0, one launch (start us, length us, event | category | flops | bytes accessed | tf_op | source)
XLA Modules:
  0.0 78.7 jit_solution(2639425945230435812)
XLA Ops:
  0.0 12.7 %copy.13.gate_hbm = bf16[5120,864]{1,0:T(8,128)(2,1)} copy(bf16[5120,864]{0,1:T(8,128)(2,1)} %param.21) | data formatting | bytes 17694720 | tf_op args[9]
  12.7 12.7 %copy.14.up_hbm = bf16[5120,864]{1,0:T(8,128)(2,1)} copy(bf16[5120,864]{0,1:T(8,128)(2,1)} %param.22) | data formatting | bytes 17694720 | tf_op args[10]
  25.4 52.0 %layer.1 = bf16[2,5120]{1,0:T(2,128)(2,1)} custom-call(s32[13]{0:T(128)} %parents.1, s32[13]{0:T(128)} %lengths.1, s32[1,64]{1,0:T(1,128)} %bitcast.3, bf16[2,5120]{1,0:T(2,128)(2,1)} %act.1, bf16[8,1280]{1,0:T(8,128)(2,1)} %query.1, f32[1,5120]{1,0:T(1,128)} %bitcast.2, bf16[1024,256]{1,0:T(8,128)(2,1)} %keys_hbm.1, bf16[1024,256]{1,0:T(8,128)(2,1)} %values_hbm.1, ...), custom_call_target="tpu_custom_call" | custom-call | tf_op jit(solution)/shard_map/layer/pallas_call | solution.py:398
  77.4 1.3 %copy.16 = bf16[2,5120]{1,0:T(2,128)(2,1)} copy(bf16[2,5120]{1,0:T(2,128)(2,1)} %layer.1) | data formatting | bytes 40960

commit v2 on v1

--- a/solution.py
+++ b/solution.py
@@ -61,11 +61,12 @@
     p_send,
     p_recv,
     res,
-    normed,
     acc_gate,
     acc_up,
     s_send,
     s_recv,
+    g_send,
+    g_recv,
     f_send,
     f_recv,
     own,
@@ -86,6 +87,8 @@
     rk_rs,
     s_ss,
     s_rs,
+    g_ss,
+    g_rs,
     f_ss,
     f_rs,
 ):
@@ -262,76 +265,86 @@
         attended = attended + p_recv[d].astype(F32)
     res[k_me, t_me] = (before + attended).astype(BF16)
 
+    block = res.at[k_me, t_me]
     for d in range(1, nt):
-        block = res.at[k_me, t_me]
         send(block, block, rt_ss.at[d], rt_rs.at[d], "tp", tp_to[d])
-    for d in range(1, nt):
-        block = res.at[k_me, tp_from[d]]
-        copy_to(block, block, rt_ss.at[d], rt_rs.at[d], "tp", tp_to[d]).wait_recv()
-    for d in range(1, nk):
-        send(res.at[k_me], res.at[k_me], rk_ss.at[d], rk_rs.at[d], "kv", kv_to[d])
-    loads[3].wait()
-    loads[4].wait()
+    for e in range(nt):
+        block = res.at[k_me, tp_from[e]]
+        if e > 0:
+            copy_to(block, block, rt_ss.at[e], rt_rs.at[e], "tp", tp_to[e]).wait_recv()
+        for d in range(1, nk):
+            send(block, block, rk_ss.at[e, d], rk_rs.at[e, d], "kv", kv_to[d])
+
+    square = jnp.zeros((tokens, 1), F32)
+    for e in range(nt):
+        c = tp_from[e]
+        for d in range(1, nk):
+            block = res.at[kv_from[d], c]
+            copy_to(block, block, rk_ss.at[e, d], rk_rs.at[e, d], "kv", kv_to[d]).wait_recv()
+        at = pl.ds(pl.multiple_of(c * cols, 128), cols)
+        part = res[:, c].astype(F32).reshape(tokens, cols)
+        square = square + jnp.sum(part * part, axis=1, keepdims=True)
+        x = (part * gain[:, at]).astype(BF16)
+        for load, weight, acc in ((loads[3], gate_w, acc_gate), (loads[4], up_w, acc_up)):
+            if e == 0:
+                load.wait()
+            product = lax.dot_general(
+                x, weight[:, at], (((1,), (1,)), ((), ())), preferred_element_type=F32
+            )
+            acc[...] = product if e == 0 else acc[...] + product
+    inverse = lax.rsqrt(square / width + EPSILON)
+    gate = acc_gate[...] * inverse
+    hidden = (gate / (1.0 + jnp.exp(-gate)) * (acc_up[...] * inverse)).astype(BF16)
     loads[5].wait()
-    acc_gate[...] = jnp.zeros_like(acc_gate)
-    acc_up[...] = jnp.zeros_like(acc_up)
-    for d in range(1, nk):
-        block = res.at[kv_from[d]]
-        copy_to(block, block, rk_ss.at[d], rk_rs.at[d], "kv", kv_to[d]).wait_recv()
-
-    for p in range(nk // 2):
-        pair = [
-            res[2 * p : 2 * p + 2, c].astype(F32).reshape(2 * group, cols) for c in range(nt)
-        ]
-        square = sum(jnp.sum(part * part, axis=1, keepdims=True) for part in pair)
-        inverse = lax.rsqrt(square / width + EPSILON)
-        for c in range(nt):
-            at = slice(c * cols, (c + 1) * cols)
-            normed[2 * p * group : 2 * (p + 1) * group, at] = (
-                pair[c] * inverse * gain[:, at]
-            ).astype(BF16)
-
-    step = 640
-
-    @pl.loop(0, width // step)
-    def _(i):
-        at = pl.ds(pl.multiple_of(i * step, 128), step)
-        x = normed[:, at]
-        acc_gate[...] += jnp.dot(x, gate_w[at, :], preferred_element_type=F32)
-        acc_up[...] += jnp.dot(x, up_w[at, :], preferred_element_type=F32)
-
-    gate = acc_gate[...]
-    hidden = (gate / (1.0 + jnp.exp(-gate)) * acc_up[...]).astype(BF16)
-
+
+    half = nk // 2
+    odd = lax.rem(k_me, 2)
+    m_me = k_me // 2
+    partner = k_me + 1 - 2 * odd
+    m_to = [lax.rem(m_me + d, half) for d in range(half)]
     chunk = width // parts
-    for c in range(parts):
-        at = slice(c * chunk, (c + 1) * chunk)
-        product = jnp.dot(hidden, down_w[:, at], preferred_element_type=F32)
-        s_send[c] = product.reshape(nk, group, chunk).astype(BF16)
-        for d in range(1, nk):
-            send(
-                s_send.at[c, kv_to[d]],
-                s_recv.at[c, d],
-                s_ss.at[c, d],
-                s_rs.at[c, d],
-                "kv",
-                kv_to[d],
+
+    def to_partner(c):
+        return copy_to(
+            s_send.at[c, 1 - odd], s_recv.at[c], s_ss.at[c], s_rs.at[c], "kv", partner
+        )
+
+    def to_others(c, d):
+        return copy_to(
+            g_send.at[c, m_to[d]],
+            g_recv.at[c, d],
+            g_ss.at[c, d],
+            g_rs.at[c, d],
+            "kv",
+            2 * m_to[d] + odd,
+        )
+
+    for c in range(parts + 1):
+        if c < parts:
+            product = jnp.dot(
+                hidden, down_w[:, c * chunk : (c + 1) * chunk], preferred_element_type=F32
+            ).reshape(half, 2, group, chunk)
+            s_send[c, 0] = product[:, 0].astype(BF16)
+            s_send[c, 1] = product[:, 1].astype(BF16)
+            copy = to_partner(c)
+            copy.start()
+            sends.append(copy)
+        if c > 0:
+            to_partner(c - 1).wait_recv()
+            g_send[c - 1] = (s_send[c - 1, odd].astype(F32) + s_recv[c - 1].astype(F32)).astype(
+                BF16
             )
+            for d in range(1, half):
+                copy = to_others(c - 1, d)
+                copy.start()
+                sends.append(copy)
 
     row = lax.broadcasted_iota(jnp.int32, (group, cols), 0)
     for c in range(parts):
-        at = slice(c * chunk, (c + 1) * chunk)
-        mixed = s_send[c, k_me].astype(F32)
-        for d in range(1, nk):
-            copy_to(
-                s_send.at[c, kv_to[d]],
-                s_recv.at[c, d],
-                s_ss.at[c, d],
-                s_rs.at[c, d],
-                "kv",
-                kv_to[d],
-            ).wait_recv()
-            mixed = mixed + s_recv[c, d].astype(F32)
+        mixed = g_send[c, m_me].astype(F32)
+        for d in range(1, half):
+            to_others(c, d).wait_recv()
+            mixed = mixed + g_recv[c, d].astype(F32)
         for t in range(nt):
             f_send[c, t] = mixed[t * rows_own : (t + 1) * rows_own].astype(BF16)
         for d in range(1, nt):
@@ -363,7 +376,7 @@
                 tp_to[d],
             ).wait_recv()
             total = total + f_recv[c, d].astype(F32)
-        result[:, at] = total.astype(BF16)
+        result[:, at] = total
     for copy in sends:
         copy.wait_send()
 
@@ -389,7 +402,7 @@
     tokens = nk * group
     cols = width // nt
     units = gate_weight.shape[1]
-    parts = 2
+    parts = 4
     chunk = width // parts
     dma = pltpu.SemaphoreType.DMA
     vmem = pl.BlockSpec(memory_space=pltpu.VMEM)
@@ -397,15 +410,15 @@
     anywhere = pl.BlockSpec(memory_space=pl.ANY)
     return pl.pallas_call(
         functools.partial(layer_kernel, nk, nt, parts),
-        out_shape=jax.ShapeDtypeStruct((rows_own, width), BF16),
+        out_shape=jax.ShapeDtypeStruct((rows_own, width), F32),
         in_specs=[smem, smem, vmem, vmem, vmem, vmem] + [anywhere] * 6,
         out_specs=vmem,
         scratch_shapes=[
             pltpu.VMEM(tree_cache_keys.shape, BF16),
             pltpu.VMEM(tree_cache_values.shape, BF16),
             pltpu.VMEM(out_weight.shape, BF16),
-            pltpu.VMEM(gate_weight.shape, BF16),
-            pltpu.VMEM(up_weight.shape, BF16),
+            pltpu.VMEM((units, width), BF16),
+            pltpu.VMEM((units, width), BF16),
             pltpu.VMEM(down_weight.shape, BF16),
             pltpu.VMEM((nk, group, q_width), BF16),
             pltpu.VMEM((nt, rows_own, width), F32),
@@ -416,11 +429,12 @@
             pltpu.VMEM((nt, group, cols), BF16),
             pltpu.VMEM((nt, group, cols), BF16),
             pltpu.VMEM((nk, nt, group, cols), BF16),
-            pltpu.VMEM((tokens, width), BF16),
             pltpu.VMEM((tokens, units), F32),
             pltpu.VMEM((tokens, units), F32),
-            pltpu.VMEM((parts, nk, group, chunk), BF16),
-            pltpu.VMEM((parts, nk, group, chunk), BF16),
+            pltpu.VMEM((parts, 2, nk // 2, group, chunk), BF16),
+            pltpu.VMEM((parts, nk // 2, group, chunk), BF16),
+            pltpu.VMEM((parts, nk // 2, group, chunk), BF16),
+            pltpu.VMEM((parts, nk // 2, group, chunk), BF16),
             pltpu.VMEM((parts, nt, rows_own, chunk), BF16),
             pltpu.VMEM((parts, nt, rows_own, chunk), BF16),
             pltpu.VMEM((rows_own, width), F32),
@@ -437,10 +451,12 @@
             dma((nt,)),
             dma((nt,)),
             dma((nt,)),
-            dma((nk,)),
-            dma((nk,)),
-            dma((parts, nk)),
-            dma((parts, nk)),
+            dma((nt, nk)),
+            dma((nt, nk)),
+            dma((parts,)),
+            dma((parts,)),
+            dma((parts, nk // 2)),
+            dma((parts, nk // 2)),
             dma((parts, nt)),
             dma((parts, nt)),
         ],
@@ -458,10 +474,10 @@
         tree_cache_keys,
         tree_cache_values,
         out_weight,
-        gate_weight,
-        up_weight,
+        gate_weight.T,
+        up_weight.T,
         down_weight,
-    )
+    ).astype(BF16)
 
 
 def solution(mesh):

time: 79.5 us -> 47.9 us (0.60)
  local copies, waits for them, and re-layouts: 26.7 us -> 0 us
  Pallas kernels: 52 us -> 46.3 us
  other arithmetic: 0 us -> 1.4 us
    unnamed x3 -> x0, local copies, waits for them, and re-layouts: 26.7 us -> none
    pallas_call x1, Pallas kernels: 52 us -> 46.3 us  [local(): pl.pallas_call(functools.partial(layer_kernel, nk, nt, parts), out_shape=...]
    convert_element_type x0 -> x1, other arithmetic: none -> 1.4 us  [local(): return pl.pallas_call(functools.partial(layer_kernel, nk, nt, parts), out...]
where the time goes in v2:
time: 47.9 us; the launch traced here: 47.7 us
  Pallas kernels  46.3 us (97%)
  other arithmetic  1.4 us (3%)
    pallas_call x1, Pallas kernels, local(): pl.pallas_call(functools.partial(layer_kernel, nk, nt, parts), out_shape=...  46.3 us
    convert_element_type x1, other arithmetic, local(): return pl.pallas_call(functools.partial(layer_kernel, nk, nt, parts), out...  1.4 us

profile of v2, /device:TPU:0, one launch (start us, length us, event | category | flops | bytes accessed | tf_op | source)
XLA Modules:
  0.0 47.7 jit_solution(10305327657669720966)
XLA Ops:
  0.0 46.3 %layer.1 = f32[2,5120]{1,0:T(2,128)} custom-call(s32[13]{0:T(128)} %parents.1, s32[13]{0:T(128)} %lengths.1, s32[1,64]{1,0:T(1,128)} %bitcast.7, bf16[2,5120]{1,0:T(2,128)(2,1)} %act.1, bf16[8,1280]{1,0:T(8,128)(2,1)} %query.1, f32[1,5120]{1,0:T(1,128)} %bitcast.6, bf16[1024,256]{1,0:T(8,128)(2,1)} %keys_hbm.1, bf16[1024,256]{1,0:T(8,128)(2,1)} %values_hbm.1, ...), custom_call_target="tpu_custom_call" | custom-call | tf_op jit(solution)/shard_map/layer/pallas_call | solution.py:411
  46.3 1.4 %convert_element_type.3 = bf16[2,5120]{1,0:T(2,128)(2,1)} convert(f32[2,5120]{1,0:T(2,128)} %layer.1) | non-fusion elementwise | flops 10240 | bytes 61440 | tf_op jit(solution)/shard_map/convert_element_type | solution.py:480

commit v3 on v2

--- a/solution.py
+++ b/solution.py
@@ -85,6 +85,8 @@
     rt_rs,
     rk_ss,
     rk_rs,
+    rp_ss,
+    rp_rs,
     s_ss,
     s_rs,
     g_ss,
@@ -137,6 +139,12 @@
     kv_from = [lax.rem(k_me + nk - d, nk) for d in range(nk)]
     tp_to = [lax.rem(t_me + d, nt) for d in range(nt)]
     tp_from = [lax.rem(t_me + nt - d, nt) for d in range(nt)]
+    half = nk // 2
+    odd = lax.rem(k_me, 2)
+    m_me = k_me // 2
+    partner = k_me + 1 - 2 * odd
+    m_to = [lax.rem(m_me + d, half) for d in range(half)]
+    m_from = [lax.rem(m_me + half - d, half) for d in range(half)]
     sends = []
 
     def send(*args):
@@ -168,7 +176,7 @@
     tenant = jnp.zeros_like(leaf)
     for n in range(nodes):
         tenant = tenant + jnp.where(leaf == n, parents[n], 0)
-    allowed = ((node == 0) | (node == tenant) | (node == leaf))[None]
+    bias = jnp.where((node == 0) | (node == tenant) | (node == leaf), 0.0, LOWEST)[None]
 
     loads[0].wait()
     loads[1].wait()
@@ -193,9 +201,9 @@
         scores = lax.dot_general(
             stacked, keys[:, head], (((1,), (1,)), ((), ())), preferred_element_type=F32
         ) * (1.0 / math.sqrt(HEAD_WIDTH))
-        scores = scores.reshape(per_kv, tokens, slots)
-        top = jnp.max(jnp.where(allowed, scores, LOWEST), axis=2, keepdims=True)
-        weights = jnp.where(allowed, jnp.exp(jnp.minimum(scores - top, 0.0)), 0.0)
+        scores = scores.reshape(per_kv, tokens, slots) + bias
+        top = jnp.max(scores, axis=2, keepdims=True)
+        weights = jnp.exp(scores - top)
         total = jnp.sum(weights, axis=2, keepdims=True)
         weighted = jnp.dot(
             weights.astype(BF16).reshape(per_kv * tokens, slots),
@@ -204,25 +212,40 @@
         ).reshape(per_kv, nk, group, HEAD_WIDTH)
         for g in range(per_kv):
             h = j * per_kv + g
-            w_send[:, :, h * HEAD_WIDTH : (h + 1) * HEAD_WIDTH] = weighted[g].astype(BF16)
+            w_send[j, :, :, g * HEAD_WIDTH : (g + 1) * HEAD_WIDTH] = weighted[g].astype(BF16)
             tops = jnp.where(lane == h, top[g], tops)
             sums = jnp.where(lane == h, total[g], sums)
-    ml_send[:, 0] = tops.reshape(nk, group, HEAD_WIDTH)
-    ml_send[:, 1] = sums.reshape(nk, group, HEAD_WIDTH)
-
-    for d in range(1, nk):
-        send(ml_send.at[kv_to[d]], ml_recv.at[d], ml_ss.at[d], ml_rs.at[d], "kv", kv_to[d])
-        send(w_send.at[kv_to[d]], w_recv.at[d], w_ss.at[d], w_rs.at[d], "kv", kv_to[d])
+        if j == kv_local - 1:
+            ml_send[:, 0] = tops.reshape(nk, group, HEAD_WIDTH)
+            ml_send[:, 1] = sums.reshape(nk, group, HEAD_WIDTH)
+            for d in range(1, nk):
+                send(ml_send.at[kv_to[d]], ml_recv.at[d], ml_ss.at[d], ml_rs.at[d], "kv", kv_to[d])
+        for d in range(1, nk):
+            send(
+                w_send.at[j, kv_to[d]],
+                w_recv.at[j, d],
+                w_ss.at[j, d],
+                w_rs.at[j, d],
+                "kv",
+                kv_to[d],
+            )
     ml_recv[0] = ml_send[k_me]
-    w_recv[0] = w_send[k_me]
+    for j in range(kv_local):
+        w_recv[j, 0] = w_send[j, k_me]
     loads[2].wait()
     for d in range(1, nk):
         copy_to(
             ml_send.at[kv_to[d]], ml_recv.at[d], ml_ss.at[d], ml_rs.at[d], "kv", kv_to[d]
         ).wait_recv()
-        copy_to(
-            w_send.at[kv_to[d]], w_recv.at[d], w_ss.at[d], w_rs.at[d], "kv", kv_to[d]
-        ).wait_recv()
+        for j in range(kv_local):
+            copy_to(
+                w_send.at[j, kv_to[d]],
+                w_recv.at[j, d],
+                w_ss.at[j, d],
+                w_rs.at[j, d],
+                "kv",
+                kv_to[d],
+            ).wait_recv()
     highest = ml_recv[0, 0]
     for d in range(1, nk):
         highest = jnp.maximum(highest, ml_recv[d, 0])
@@ -233,8 +256,9 @@
     pieces = []
     for h in range(kv_local * per_kv):
         total = jnp.zeros((group, HEAD_WIDTH), F32)
+        j, g = divmod(h, per_kv)
         for d in range(nk):
-            part = w_recv[d, :, h * HEAD_WIDTH : (h + 1) * HEAD_WIDTH].astype(F32)
+            part = w_recv[j, d, :, g * HEAD_WIDTH : (g + 1) * HEAD_WIDTH].astype(F32)
             total = total + part * scales[d][:, h : h + 1]
         pieces.append(total / denominator[:, h : h + 1])
     context = jnp.concatenate(pieces, axis=1).astype(BF16)
@@ -272,15 +296,25 @@
         block = res.at[k_me, tp_from[e]]
         if e > 0:
             copy_to(block, block, rt_ss.at[e], rt_rs.at[e], "tp", tp_to[e]).wait_recv()
-        for d in range(1, nk):
-            send(block, block, rk_ss.at[e, d], rk_rs.at[e, d], "kv", kv_to[d])
+        send(block, block, rp_ss.at[e, 0], rp_rs.at[e, 0], "kv", partner)
+        for d in range(1, half):
+            send(block, block, rk_ss.at[e, d], rk_rs.at[e, d], "kv", 2 * m_to[d] + odd)
+
+    def forward(e):
+        for d in range(1, half):
+            block = res.at[2 * m_from[d] + odd, tp_from[e]]
+            copy_to(
+                block, block, rk_ss.at[e, d], rk_rs.at[e, d], "kv", 2 * m_to[d] + odd
+            ).wait_recv()
+            send(block, block, rp_ss.at[e, d], rp_rs.at[e, d], "kv", partner)
 
     square = jnp.zeros((tokens, 1), F32)
+    forward(0)
     for e in range(nt):
         c = tp_from[e]
-        for d in range(1, nk):
-            block = res.at[kv_from[d], c]
-            copy_to(block, block, rk_ss.at[e, d], rk_rs.at[e, d], "kv", kv_to[d]).wait_recv()
+        for d in range(half):
+            block = res.at[2 * m_from[d] + 1 - odd, c]
+            copy_to(block, block, rp_ss.at[e, d], rp_rs.at[e, d], "kv", partner).wait_recv()
         at = pl.ds(pl.multiple_of(c * cols, 128), cols)
         part = res[:, c].astype(F32).reshape(tokens, cols)
         square = square + jnp.sum(part * part, axis=1, keepdims=True)
@@ -292,16 +326,13 @@
                 x, weight[:, at], (((1,), (1,)), ((), ())), preferred_element_type=F32
             )
             acc[...] = product if e == 0 else acc[...] + product
+            if acc is acc_gate and e + 1 < nt:
+                forward(e + 1)
     inverse = lax.rsqrt(square / width + EPSILON)
     gate = acc_gate[...] * inverse
     hidden = (gate / (1.0 + jnp.exp(-gate)) * (acc_up[...] * inverse)).astype(BF16)
     loads[5].wait()
 
-    half = nk // 2
-    odd = lax.rem(k_me, 2)
-    m_me = k_me // 2
-    partner = k_me + 1 - 2 * odd
-    m_to = [lax.rem(m_me + d, half) for d in range(half)]
     chunk = width // parts
 
     def to_partner(c):
@@ -402,6 +433,7 @@
     tokens = nk * group
     cols = width // nt
     units = gate_weight.shape[1]
+    kv_local = tree_cache_keys.shape[1] // HEAD_WIDTH
     parts = 4
     chunk = width // parts
     dma = pltpu.SemaphoreType.DMA
@@ -422,8 +454,8 @@
             pltpu.VMEM(down_weight.shape, BF16),
             pltpu.VMEM((nk, group, q_width), BF16),
             pltpu.VMEM((nt, rows_own, width), F32),
-            pltpu.VMEM((nk, group, q_width), BF16),
-            pltpu.VMEM((nk, group, q_width), BF16),
+            pltpu.VMEM((kv_local, nk, group, q_width // kv_local), BF16),
+            pltpu.VMEM((kv_local, nk, group, q_width // kv_local), BF16),
             pltpu.VMEM((nk, 2, group, HEAD_WIDTH), F32),
             pltpu.VMEM((nk, 2, group, HEAD_WIDTH), F32),
             pltpu.VMEM((nt, group, cols), BF16),
@@ -443,16 +475,18 @@
             dma((nk,)),
             dma((nt,)),
             dma((nt,)),
-            dma((nk,)),
-            dma((nk,)),
+            dma((kv_local, nk)),
+            dma((kv_local, nk)),
             dma((nk,)),
             dma((nk,)),
             dma((nt,)),
             dma((nt,)),
             dma((nt,)),
             dma((nt,)),
-            dma((nt, nk)),
-            dma((nt, nk)),
+            dma((nt, nk // 2)),
+            dma((nt, nk // 2)),
+            dma((nt, nk // 2)),
+            dma((nt, nk // 2)),
             dma((parts,)),
             dma((parts,)),
             dma((parts, nk // 2)),

time: 47.9 us -> 48.7 us (1.017)
  Pallas kernels: 46.3 us -> 47 us
    pallas_call x1, Pallas kernels: 46.3 us -> 47 us  [local(): pl.pallas_call(functools.partial(layer_kernel, nk, nt, parts), out_shape=...]
where the time goes in v3:
time: 48.7 us; the launch traced here: 48.4 us
  Pallas kernels  47 us (97%)
  other arithmetic  1.4 us (3%)
    pallas_call x1, Pallas kernels, local(): pl.pallas_call(functools.partial(layer_kernel, nk, nt, parts), out_shape=...  47 us
    convert_element_type x1, other arithmetic, local(): return pl.pallas_call(functools.partial(layer_kernel, nk, nt, parts), out...  1.4 us

profile of v3, /device:TPU:0, one launch (start us, length us, event | category | flops | bytes accessed | tf_op | source)
XLA Modules:
  0.0 48.4 jit_solution(17269012192589850484)
XLA Ops:
  0.0 47.0 %layer.1 = f32[2,5120]{1,0:T(2,128)} custom-call(s32[13]{0:T(128)} %parents.1, s32[13]{0:T(128)} %lengths.1, s32[1,64]{1,0:T(1,128)} %bitcast.7, bf16[2,5120]{1,0:T(2,128)(2,1)} %act.1, bf16[8,1280]{1,0:T(8,128)(2,1)} %query.1, f32[1,5120]{1,0:T(1,128)} %bitcast.6, bf16[1024,256]{1,0:T(8,128)(2,1)} %keys_hbm.1, bf16[1024,256]{1,0:T(8,128)(2,1)} %values_hbm.1, ...), custom_call_target="tpu_custom_call" | custom-call | tf_op jit(solution)/shard_map/layer/pallas_call | solution.py:443
  47.0 1.4 %convert_element_type.3 = bf16[2,5120]{1,0:T(2,128)(2,1)} convert(f32[2,5120]{1,0:T(2,128)} %layer.1) | non-fusion elementwise | flops 10240 | bytes 61440 | tf_op jit(solution)/shard_map/convert_element_type | solution.py:514

commit v4 on v2

--- a/solution.py
+++ b/solution.py
@@ -16,6 +16,7 @@
 MESH = pl.DeviceIdType.MESH
 F32 = jnp.float32
 BF16 = jnp.bfloat16
+LOAD_PIECES = 2
 
 
 def copy_to(source, target, send, receive, axis, peer):
@@ -103,21 +104,39 @@
     rows_own = act.shape[0]
     cols = width // nt
 
-    loads = [
-        pltpu.make_async_copy(source, target, load_sem.at[i])
-        for i, (source, target) in enumerate(
-            (
-                (keys_hbm, keys),
-                (values_hbm, values),
-                (out_hbm, out_w),
-                (gate_hbm, gate_w),
-                (up_hbm, up_w),
-                (down_hbm, down_w),
-            )
+    loads = []
+    for source, target in (
+        (keys_hbm, keys),
+        (values_hbm, values),
+        (out_hbm, out_w),
+        (gate_hbm, gate_w),
+        (up_hbm, up_w),
+        (down_hbm, down_w),
+    ):
+        rows = source.shape[0]
+        pieces = LOAD_PIECES if rows % (LOAD_PIECES * 16) == 0 else 1
+        size = rows // pieces
+        loads.append(
+            [
+                pltpu.make_async_copy(
+                    source.at[pl.ds(i * size, size)],
+                    target.at[pl.ds(i * size, size)],
+                    load_sem.at[len(loads), i],
+                )
+                for i in range(pieces)
+            ]
         )
-    ]
-    for load in loads:
-        load.start()
+
+    def start(which):
+        for copy in loads[which]:
+            copy.start()
+
+    def loaded(which):
+        for copy in loads[which]:
+            copy.wait()
+
+    for which in range(3):
+        start(which)
 
     q_all[k_me] = query[...]
     act_all[t_me] = act[...].astype(F32)
@@ -168,13 +187,16 @@
     tenant = jnp.zeros_like(leaf)
     for n in range(nodes):
         tenant = tenant + jnp.where(leaf == n, parents[n], 0)
-    allowed = ((node == 0) | (node == tenant) | (node == leaf))[None]
-
-    loads[0].wait()
-    loads[1].wait()
+    bias = jnp.where((node == 0) | (node == tenant) | (node == leaf), 0.0, LOWEST)[None]
+
+    loaded(0)
+    loaded(1)
     for d in range(1, nk):
         block = q_all.at[kv_from[d]]
         copy_to(block, block, q_ss.at[d], q_rs.at[d], "kv", kv_to[d]).wait_recv()
+
+    for which in range(3, 6):
+        start(which)
 
     lane = lax.broadcasted_iota(jnp.int32, (tokens, HEAD_WIDTH), 1)
     tops = jnp.zeros((tokens, HEAD_WIDTH), F32)
@@ -193,9 +215,9 @@
         scores = lax.dot_general(
             stacked, keys[:, head], (((1,), (1,)), ((), ())), preferred_element_type=F32
         ) * (1.0 / math.sqrt(HEAD_WIDTH))
-        scores = scores.reshape(per_kv, tokens, slots)
-        top = jnp.max(jnp.where(allowed, scores, LOWEST), axis=2, keepdims=True)
-        weights = jnp.where(allowed, jnp.exp(jnp.minimum(scores - top, 0.0)), 0.0)
+        scores = scores.reshape(per_kv, tokens, slots) + bias
+        top = jnp.max(scores, axis=2, keepdims=True)
+        weights = jnp.exp(scores - top)
         total = jnp.sum(weights, axis=2, keepdims=True)
         weighted = jnp.dot(
             weights.astype(BF16).reshape(per_kv * tokens, slots),
@@ -215,7 +237,7 @@
         send(w_send.at[kv_to[d]], w_recv.at[d], w_ss.at[d], w_rs.at[d], "kv", kv_to[d])
     ml_recv[0] = ml_send[k_me]
     w_recv[0] = w_send[k_me]
-    loads[2].wait()
+    loaded(2)
     for d in range(1, nk):
         copy_to(
             ml_send.at[kv_to[d]], ml_recv.at[d], ml_ss.at[d], ml_rs.at[d], "kv", kv_to[d]
@@ -285,9 +307,9 @@
         part = res[:, c].astype(F32).reshape(tokens, cols)
         square = square + jnp.sum(part * part, axis=1, keepdims=True)
         x = (part * gain[:, at]).astype(BF16)
-        for load, weight, acc in ((loads[3], gate_w, acc_gate), (loads[4], up_w, acc_up)):
+        for load, weight, acc in ((3, gate_w, acc_gate), (4, up_w, acc_up)):
             if e == 0:
-                load.wait()
+                loaded(load)
             product = lax.dot_general(
                 x, weight[:, at], (((1,), (1,)), ((), ())), preferred_element_type=F32
             )
@@ -295,7 +317,7 @@
     inverse = lax.rsqrt(square / width + EPSILON)
     gate = acc_gate[...] * inverse
     hidden = (gate / (1.0 + jnp.exp(-gate)) * (acc_up[...] * inverse)).astype(BF16)
-    loads[5].wait()
+    loaded(5)
 
     half = nk // 2
     odd = lax.rem(k_me, 2)
@@ -376,9 +398,15 @@
                 tp_to[d],
             ).wait_recv()
             total = total + f_recv[c, d].astype(F32)
-        result[:, at] = total
+        result[:, at] = total.astype(BF16)
     for copy in sends:
         copy.wait_send()
+
+
+def hand_over(source, target, sem):
+    copy = pltpu.make_async_copy(source, target, sem)
+    copy.start()
+    copy.wait()
 
 
 def local(
@@ -408,9 +436,9 @@
     vmem = pl.BlockSpec(memory_space=pltpu.VMEM)
     smem = pl.BlockSpec(memory_space=pltpu.SMEM)
     anywhere = pl.BlockSpec(memory_space=pl.ANY)
-    return pl.pallas_call(
+    output = pl.pallas_call(
         functools.partial(layer_kernel, nk, nt, parts),
-        out_shape=jax.ShapeDtypeStruct((rows_own, width), F32),
+        out_shape=jax.ShapeDtypeStruct((rows_own, width), BF16),
         in_specs=[smem, smem, vmem, vmem, vmem, vmem] + [anywhere] * 6,
         out_specs=vmem,
         scratch_shapes=[
@@ -438,7 +466,7 @@
             pltpu.VMEM((parts, nt, rows_own, chunk), BF16),
             pltpu.VMEM((parts, nt, rows_own, chunk), BF16),
             pltpu.VMEM((rows_own, width), F32),
-            dma((6,)),
+            dma((6, LOAD_PIECES)),
             dma((nk,)),
             dma((nk,)),
             dma((nt,)),
@@ -477,7 +505,15 @@
         gate_weight.T,
         up_weight.T,
         down_weight,
-    ).astype(BF16)
+    )
+    return pl.pallas_call(
+        hand_over,
+        out_shape=jax.ShapeDtypeStruct(output.shape, BF16),
+        in_specs=[pl.BlockSpec(memory_space=pltpu.HBM)],
+        out_specs=pl.BlockSpec(memory_space=pltpu.HBM),
+        scratch_shapes=[dma],
+        name="hand_over",
+    )(output)
 
 
 def solution(mesh):

time: 47.9 us -> 47.9 us (level)
  Pallas kernels: 46.3 us -> 47.7 us
  other arithmetic: 1.4 us -> 0 us
    pallas_call x0 -> x1, Pallas kernels: none -> 1.73 us  [local(): pl.pallas_call(hand_over, out_shape=jax.ShapeDtypeStruct(output.shape, BF...]
    convert_element_type x1 -> x0, other arithmetic: 1.4 us -> none  [local(): return pl.pallas_call(functools.partial(layer_kernel, nk, nt, parts), out...]
where the time goes in v4:
time: 47.9 us; the launch traced here: 47.7 us
  Pallas kernels  47.7 us (100%)
    pallas_call x1, Pallas kernels, local(): pl.pallas_call(functools.partial(layer_kernel, nk, nt, parts), out_shape=...  46 us
    pallas_call x1, Pallas kernels, local(): pl.pallas_call(hand_over, out_shape=jax.ShapeDtypeStruct(output.shape, BF...  1.73 us

profile of v4, /device:TPU:0, one launch (start us, length us, event | category | flops | bytes accessed | tf_op | source)
XLA Modules:
  0.0 47.7 jit_solution(14126342158993106041)
XLA Ops:
  0.0 46.0 %layer.1.source = bf16[2,5120]{1,0:T(2,128)(2,1)} custom-call(s32[13]{0:T(128)} %parents.1, s32[13]{0:T(128)} %lengths.1, s32[1,64]{1,0:T(1,128)} %bitcast.7, bf16[2,5120]{1,0:T(2,128)(2,1)} %act.1, bf16[8,1280]{1,0:T(8,128)(2,1)} %query.1, f32[1,5120]{1,0:T(1,128)} %bitcast.6, bf16[1024,256]{1,0:T(8,128)(2,1)} %keys_hbm.1, bf16[1024,256]{1,0:T(8,128)(2,1)} %values_hbm.1, ...), custom_call_target="tpu_custom_call" | custom-call | tf_op jit(solution)/shard_map/layer/pallas_call | solution.py:439
  46.0 1.7 %hand_over.1 = bf16[2,5120]{1,0:T(2,128)(2,1)} custom-call(bf16[2,5120]{1,0:T(2,128)(2,1)} %layer.1.source), custom_call_target="tpu_custom_call" | custom-call | tf_op jit(solution)/shard_map/hand_over/pallas_call | solution.py:509

commit v5 on v4

--- a/solution.py
+++ b/solution.py
@@ -398,15 +398,9 @@
                 tp_to[d],
             ).wait_recv()
             total = total + f_recv[c, d].astype(F32)
-        result[:, at] = total.astype(BF16)
+        result[:, at] = total
     for copy in sends:
         copy.wait_send()
-
-
-def hand_over(source, target, sem):
-    copy = pltpu.make_async_copy(source, target, sem)
-    copy.start()
-    copy.wait()
 
 
 def local(
@@ -430,7 +424,7 @@
     tokens = nk * group
     cols = width // nt
     units = gate_weight.shape[1]
-    parts = 4
+    parts = 2
     chunk = width // parts
     dma = pltpu.SemaphoreType.DMA
     vmem = pl.BlockSpec(memory_space=pltpu.VMEM)
@@ -438,7 +432,7 @@
     anywhere = pl.BlockSpec(memory_space=pl.ANY)
     output = pl.pallas_call(
         functools.partial(layer_kernel, nk, nt, parts),
-        out_shape=jax.ShapeDtypeStruct((rows_own, width), BF16),
+        out_shape=jax.ShapeDtypeStruct((rows_own, width), F32),
         in_specs=[smem, smem, vmem, vmem, vmem, vmem] + [anywhere] * 6,
         out_specs=vmem,
         scratch_shapes=[
@@ -506,14 +500,7 @@
         up_weight.T,
         down_weight,
     )
-    return pl.pallas_call(
-        hand_over,
-        out_shape=jax.ShapeDtypeStruct(output.shape, BF16),
-        in_specs=[pl.BlockSpec(memory_space=pltpu.HBM)],
-        out_specs=pl.BlockSpec(memory_space=pltpu.HBM),
-        scratch_shapes=[dma],
-        name="hand_over",
-    )(output)
+    return output.astype(BF16)
 
 
 def solution(mesh):

time: 47.9 us -> 47.8 us (level)
  Pallas kernels: 47.7 us -> 46.2 us
  other arithmetic: 0 us -> 1.4 us
    pallas_call x1 -> x0, Pallas kernels: 1.73 us -> none  [local(): pl.pallas_call(hand_over, out_shape=jax.ShapeDtypeStruct(output.shape, BF...]
    convert_element_type x0 -> x1, other arithmetic: none -> 1.4 us  [local(): return output.astype(BF16)]
where the time goes in v5:
time: 47.8 us; the launch traced here: 47.6 us
  Pallas kernels  46.2 us (97%)
  other arithmetic  1.4 us (3%)
    pallas_call x1, Pallas kernels, local(): pl.pallas_call(functools.partial(layer_kernel, nk, nt, parts), out_shape=...  46.2 us
    convert_element_type x1, other arithmetic, local(): return output.astype(BF16)  1.4 us

profile of v5, /device:TPU:0, one launch (start us, length us, event | category | flops | bytes accessed | tf_op | source)
XLA Modules:
  0.0 47.6 jit_solution(6408118848649131113)
XLA Ops:
  0.0 46.2 %layer.1 = f32[2,5120]{1,0:T(2,128)} custom-call(s32[13]{0:T(128)} %parents.1, s32[13]{0:T(128)} %lengths.1, s32[1,64]{1,0:T(1,128)} %bitcast.7, bf16[2,5120]{1,0:T(2,128)(2,1)} %act.1, bf16[8,1280]{1,0:T(8,128)(2,1)} %query.1, f32[1,5120]{1,0:T(1,128)} %bitcast.6, bf16[1024,256]{1,0:T(8,128)(2,1)} %keys_hbm.1, bf16[1024,256]{1,0:T(8,128)(2,1)} %values_hbm.1, ...), custom_call_target="tpu_custom_call" | custom-call | tf_op jit(solution)/shard_map/layer/pallas_call | solution.py:433
  46.2 1.4 %convert_element_type.3 = bf16[2,5120]{1,0:T(2,128)(2,1)} convert(f32[2,5120]{1,0:T(2,128)} %layer.1) | non-fusion elementwise | flops 10240 | bytes 61440 | tf_op jit(solution)/shard_map/convert_element_type | solution.py:503
